TPU v7x, 256 devices: a whole 4x4x8 slice. The times are simulated.
256 devices in a mesh: feat: 8 (over x, z_hi), store: 32 (over y, z_lo, core).
Axes of the slice: x: 4, y: 4, z: 8 (z_hi: 2, z_lo: 4; z = z_hi * 4 + z_lo), core: 2. Of those that a mesh axis runs over, the one named last changes fastest.
Arguments:
- layer_input: bfloat16 [16384, 8192], P('store', 'feat'), may hold values from -6 to 6
- out_grad: bfloat16 [16384, 8192], P('store', 'feat'), may hold values from -6 to 6
- proj_in: bfloat16 [8192, 256], P('feat'), may hold values from -0.0625 to 0.0625
- proj_out: bfloat16 [8192, 256], P('feat'), may hold values from -0.0625 to 0.0625
- inv_diag: float32 [65536], P('feat'), may hold values from 0.1 to 10
- stored: float32 [6144, 65536], P('store', 'feat'), may hold values from -0.0014648438 to 0.0014648438
- seq_lengths: int32 [32, 16], P('store'), may hold values from 1 to 64, 512 in all within a row
- query_order: int32 [32, 16], P('store'), may hold values from 0 to 15, as said below
Outputs:
- scores: float32 [512, 6144], P('feat', 'store')
Inputs may be any that keep to these rules, and one draw needn't show every extreme that they name: `query_order`: each row is an ordering of the query slots 0 to 15, each slot once.
All inputs are finite; a program needn't handle non-finite values.
Results may differ from a plain program's by a relative error of at most 0.0003.
Values sent between devices are 32-bit elements; how exact they have to be, the bound alone decides.
A program may use at most 64 MiB of HBM per device.

v0:
```python
import jax
import jax.numpy as jnp
from jax import lax
from jax.sharding import PartitionSpec as P

Q_DEV = 16


def token_slots(lengths_row, order_row, count):
    ends = jnp.cumsum(lengths_row)
    position = jnp.arange(count, dtype=jnp.int32)
    segment = jnp.sum((position[:, None] >= ends[None, :]).astype(jnp.int32), axis=1)
    slots = jnp.arange(Q_DEV, dtype=jnp.int32)
    picked = (segment[:, None] == slots[None, :]).astype(jnp.int32)
    return jnp.sum(picked * order_row[None, :], axis=1)


def outer_sums(member, in_part, grad_full):
    masked = member[:, :, None] * in_part[None, :, :]
    outer = jnp.einsum("qti,tj->qij", masked, grad_full, precision=lax.Precision.HIGHEST)
    return outer.reshape(member.shape[0], -1)


def body(layer_input, out_grad, proj_in, proj_out, inv_diag, stored, seq_lengths, query_order):
    count = layer_input.shape[0]
    in_terms = jnp.dot(layer_input, proj_in, preferred_element_type=jnp.float32)
    grad_terms = jnp.dot(out_grad, proj_out, preferred_element_type=jnp.float32)
    in_part = lax.psum_scatter(in_terms, "feat", scatter_dimension=1, tiled=True)
    grad_full = lax.psum(grad_terms, "feat")
    slot_ids = token_slots(seq_lengths[0], query_order[0], count)
    slots = jnp.arange(Q_DEV, dtype=jnp.int32)
    member = (slot_ids[None, :] == slots[:, None]).astype(jnp.float32)
    query_grad = outer_sums(member, in_part, grad_full) * inv_diag[None, :]
    partial_scores = jnp.einsum(
        "qf,rf->qr",
        lax.all_gather(query_grad, "store", axis=0, tiled=True),
        stored,
        precision=lax.Precision.HIGHEST,
    )
    return lax.psum_scatter(partial_scores, "feat", scatter_dimension=0, tiled=True)


def solution(mesh):
    return jax.shard_map(
        body,
        mesh=mesh,
        in_specs=(
            P("store", "feat"),
            P("store", "feat"),
            P("feat", None),
            P("feat", None),
            P("feat"),
            P("store", "feat"),
            P("store", None),
            P("store", None),
        ),
        out_specs=P("feat", "store"),
        check_vma=False,
    )
```

profile of v0, /device:TPU:27, one launch (start us, length us, event | category | flops | bytes accessed | tf_op | source)
XLA Modules:
  0.0 415.8 jit_solution(6404235366609810418)
XLA Ops:
  6.5 0.0 copy-start
  6.5 0.0 all-reduce.2.cloned.1.call-start
  6.5 1.2 copy-done
  7.8 2.3 fusion.7
  10.1 0.0 all-reduce.2.cloned.1.call-update
  10.1 0.0 reduce-scatter.3.cloned.1.call-start
  10.1 2.7 fusion.6
  12.8 0.0 reduce-scatter.3.cloned.1.call-update
  12.8 0.0 all-gather.2.cloned.1.call-start
  12.9 0.7 copy.11
  13.6 0.1 reduce
  13.8 0.1 convert_reduce_fusion
  13.9 0.7 select_reduce_fusion
  14.6 103.0 %all-reduce.2.cloned.1.call-done = f32[512,256]{1,0:T(8,128)} async-done(((f32[512,256]{1,0:T(8,128)}), f32[512,256]{1,0:T(8,128)}) %all-reduce.2.cloned.1.call-update) | async-done | bytes 524304 | tf_op jit(solution)/shard_map/psum | solution.py:29
  117.6 88.2 %reduce-scatter.3.cloned.1.call-done = f32[512,32]{0,1:T(8,128)} async-done(((f32[512,256]{0,1:T(8,128)}), f32[512,32]{0,1:T(8,128)}) %reduce-scatter.3.cloned.1.call-update) | async-done | bytes 65552 | tf_op jit(solution)/shard_map/reduce_scatter | solution.py:28
  205.8 2.1 fusion
  207.8 0.3 copy.12
  208.2 1.6 broadcast_multiply_fusion
  209.8 0.0 all-gather.2.cloned.1.call-update
  209.8 0.0 reduce-scatter.5.cloned.1.call-start
  209.8 99.0 %all-gather.2.cloned.1.call-done = f32[512,8192]{1,0:T(8,128)} async-done(((f32[16,8192]{1,0:T(8,128)}), f32[512,8192]{1,0:T(8,128)}) %all-gather.2.cloned.1.call-update) | async-done | bytes 16777232 | tf_op jit(solution)/shard_map/all_gather | solution.py:36
  308.8 18.1 %fusion.8 = f32[512,192]{1,0:T(8,128)} fusion(f32[512,8192]{1,0:T(8,128)} %all-gather.2.cloned.1.call-done, f32[192,8192]{1,0:T(8,128)} %param.13), kind=kOutput, calls=%fused_computation.14 | convolution fusion | flops 9663676416 | bytes 23461888 | tf_op jit(solution)/shard_map/qf,rf->qr/dot_general | solution.py:34
  326.9 0.0 reduce-scatter.5.cloned.1.call-update
  326.9 82.3 %reduce-scatter.5.cloned.1.call-done = f32[64,192]{1,0:T(8,128)} async-done(((f32[512,192]{1,0:T(8,128)}), f32[64,192]{1,0:T(8,128)}) %reduce-scatter.5.cloned.1.call-update) | async-done | bytes 49168 | tf_op jit(solution)/shard_map/reduce_scatter | solution.py:40
  (2 shorter events, 0.0 us)
Async XLA Ops:
  6.5 1.2 copy-start
  6.5 111.1 %all-reduce.2.cloned.1.call-start = ((), (), s32[]{:S(2)}) async-start(), calls=%async_computation.3 | async-start | bytes 1048576 | tf_op jit(solution)/shard_map/psum | solution.py:29
  10.1 195.7 %reduce-scatter.3.cloned.1.call-start = ((), (), s32[]{:S(2)}) async-start(), calls=%async_computation.2 | async-start | bytes 589824 | tf_op jit(solution)/shard_map/reduce_scatter | solution.py:28
  12.8 296.0 %all-gather.2.cloned.1.call-start = ((), (), s32[]{:S(2)}) async-start(), calls=%async_computation.4 | async-start | bytes 17301504 | tf_op jit(solution)/shard_map/all_gather | solution.py:36
  209.8 199.5 %reduce-scatter.5.cloned.1.call-start = ((), (), s32[]{:S(2)}) async-start(), calls=%async_computation.5 | async-start | bytes 589824 | tf_op jit(solution)/shard_map/reduce_scatter | solution.py:40
Sparse Core Ops, SparseCore 0:
  10.2 107.3 all-reduce.1
  122.0 83.7 reduce-scatter.2
  209.9 98.8 all-gather.1
  327.0 82.1 reduce-scatter.4
where the time goes:
time: 419 us; the launch traced here: 416 us
  waiting for transfers between devices  373 us (89%)
  matrix products  25.1 us (6%)
  between operations  13.1 us (3%)
    psum x1, waiting for transfers between devices, body(): grad_full = lax.psum(grad_terms, 'feat')  103 us
    all_gather x1, waiting for transfers between devices, body(): lax.all_gather(query_grad, 'store', axis=0, tiled=True)  99 us
    reduce_scatter x1, waiting for transfers between devices, body(): lax.psum_scatter(in_terms, 'feat', scatter_dimension=1, tiled=True)  88.2 us
    reduce_scatter x1, waiting for transfers between devices, body(): lax.psum_scatter(partial_scores, 'feat', scatter_dimension=0, tiled=True)  82.3 us
    dot_general x1, matrix products, body(): jnp.einsum('qf,rf->qr', lax.all_gather(query_grad, 'store', axis=0, tiled...  18.1 us
  transfers between devices with their start and end apart: 4, of which 4 were waited for; matrix products, arithmetic and copies ran while one was open for 1% of the time, Pallas kernels for 0%

commit v1 on v0

v1 whole, which is shorter than its diff:
```python
import heapq

import jax
import jax.numpy as jnp
from jax import lax
from jax.experimental import pallas as pl
from jax.experimental.pallas import tpu as pltpu
from jax.sharding import PartitionSpec as P

MESH = pl.DeviceIdType.MESH
F32, BF16 = jnp.float32, jnp.bfloat16
NX, NY, NZ = 4, 4, 8
QB = 16
A0, B0, C0, TOK = 0, 16, 40, 64
INROWS = 40


def place():
    f, s = lax.axis_index("feat"), lax.axis_index("store")
    return f // 2, s // 8, (f % 2) * 4 + (s // 2) % 4, s % 2


def device(x, y, z, c):
    x, y, z, c = x % NX, y % NY, z % NZ, c % 2
    return (x * 2 + z // 4, y * 8 + (z % 4) * 2 + c)


class Message:
    def __init__(self, name, deps, kb, axis, hop, ref):
        self.name, self.deps, self.kb, self.axis, self.hop, self.ref = name, deps, kb, axis, hop, ref


def gather_plan(me, grads, ins):
    x, y, z, c = me
    out = []

    def zz(v):
        return v % 4, (v % NZ) // 4

    def add(name, deps, kb, axis, hop, ref):
        out.append(Message(name, tuple(deps), kb, axis, hop, ref))

    def ga(zv, ys=slice(None)):
        lo, hi = zz(zv)
        return grads.at[ys, lo, :, hi, A0:B0, :]

    def gb(zv, xv, ys=slice(None)):
        lo, hi = zz(zv)
        return grads.at[ys, lo, xv % NX, hi, B0:C0, :]

    def gc(xv, yv, zs=slice(None)):
        return grads.at[yv % NY, zs, xv % NX, :, C0:TOK, :]

    first, second = pl.ds(0, 2), pl.ds(2, 2)
    lo, hi = zz(z)
    for k in (1, 2, 3, 4):
        for sign in (1, -1):
            zlo, zhi = zz(z - sign * (k - 1))
            cols = slice(None) if k < 4 else pl.ds(0 if sign > 0 else 128, 128)
            deps = ["g"] if k == 1 else [f"Cz{sign * (k - 1)}"]
            add(f"Cz{sign * k}", deps, 24 if k < 4 else 12, "z", sign, grads.at[y, zlo, x, zhi, C0:TOK, cols])
    call = [f"Cz{s * k}" for k in (1, 2, 3, 4) for s in (1, -1)]
    for sign in (1, -1):
        add(f"Cx{sign}", ["g"] + call, 192, "x", sign, gc(x, y))
    for sign in (1, -1):
        add(f"Cx{2 * sign}", [f"Cx{sign}"], 96, "x", sign, gc(x - sign, y, first if sign > 0 else second))
    for hop in (1, -1, 2):
        add(f"By{hop}", ["g"], 24, "y", hop, grads.at[y, lo, x, hi, B0:C0, :])
    ball = ["g"] + [f"By{h}" for h in (1, -1, 2)]
    for k in (1, 2, 3, 4):
        for sign in (1, -1):
            deps = ball if k == 1 else [f"Bz{sign * (k - 1)}"]
            ys = slice(None) if k < 4 else (first if sign > 0 else second)
            add(f"Bz{sign * k}", deps, 96 if k < 4 else 48, "z", sign, gb(z - sign * (k - 1), x, ys))
    for hop in (1, -1, 2):
        add(f"Ax{hop}", ["g"], 16, "x", hop, grads.at[y, lo, x, hi, A0:B0, :])
    aall = ["g"] + [f"Ax{h}" for h in (1, -1, 2)]
    for hop in (1, -1, 2):
        add(f"Ay{hop}", aall, 64, "y", hop, grads.at[y, lo, :, hi, A0:B0, :])
    for k in (1, 2, 3):
        add(f"Iz{k}", ["i"], 80, "i", k, ins.at[y, lo])
    iall = ["i"] + [f"Iz{k}" for k in (1, 2, 3)]
    for sign in (1, -1):
        add(f"Iy{sign}", iall, 320, "y", sign, ins.at[y])
    for sign in (1, -1):
        add(f"Iy{2 * sign}", [f"Iy{sign}"], 160, "y", sign, ins.at[(y - sign) % NY, first if sign > 0 else second])
    for d in (0, -1, 1, -2, 2, -3, 3, 4):
        if d == 0:
            deps = ball
        elif d == 4:
            deps = ["Bz4", "Bz-4"]
        else:
            deps = [f"Bz{-d}"]
        for sign in (1, -1):
            add(f"Bx{d},{sign}", deps, 96, "x", sign, gb(z + d, x))
        for sign in (1, -1):
            add(f"Bx{d},{2 * sign}", [f"Bx{d},{sign}"], 48, "x", sign, gb(z + d, x - sign, first if sign > 0 else second))
    for d in (0, -1, 1, 2):
        deps = (["g"] + call) if d == 0 else (["Cx2", "Cx-2"] if d == 2 else [f"Cx{-d}"])
        for sign in (1, -1):
            add(f"Cy{d},{sign}", deps, 192, "y", sign, gc(x + d, y))
        for sign in (1, -1):
            add(f"Cy{d},{2 * sign}", [f"Cy{d},{sign}"], 96, "y", sign, gc(x + d, y - sign, first if sign > 0 else second))
    yall = aall + [f"Ay{h}" for h in (1, -1, 2)]
    for k in (1, 2, 3, 4):
        for sign in (1, -1):
            deps = yall if k == 1 else [f"Az{sign * (k - 1)}"]
            ys = slice(None) if k < 4 else (first if sign > 0 else second)
            add(f"Az{sign * k}", deps, 256 if k < 4 else 128, "z", sign, ga(z - sign * (k - 1), ys))
    return out


def target(me, m):
    x, y, z, c = me
    if m.axis == "x":
        return device(x + m.hop, y, z, c)
    if m.axis == "y":
        return device(x, y + m.hop, z, c)
    if m.axis == "z":
        return device(x, y, z + m.hop, c)
    return device(x, y, (z // 4) * 4 + (z % 4 + m.hop) % 4, c)


def order_of(plan, late=8.0):
    rate, latency = 42.0, 1.5
    free, got, sent, events, steps = {}, set(), set(), [(0.0, 0, "g"), (late, 1, "i")], []
    heapq.heapify(events)
    count = 2
    while events:
        now, _, name = heapq.heappop(events)
        got.add(name)
        steps.append(("wait", name))
        for m in plan:
            if m.name in sent or not all(d in got for d in m.deps):
                continue
            sent.add(m.name)
            steps.append(("send", m.name))
            if m.axis == "i":
                links, kb = ("z+", "z-"), m.kb
            elif abs(m.hop) > 1:
                links, kb = (m.axis + "+", m.axis + "-"), m.kb
            else:
                links, kb = ((m.axis + "+",) if m.hop > 0 else (m.axis + "-",)), m.kb
            end = max(now, *(free.get(k, 0.0) for k in links)) + kb / rate
            for k in links:
                free[k] = end
            heapq.heappush(events, (end + latency, count, m.name))
            count += 1
    return steps


def split(v):
    high = v.astype(BF16)
    return high, (v - high.astype(F32)).astype(BF16)


def dot3(a, b, dims):
    (ah, al), (bh, bl) = a, b
    return (
        lax.dot_general(ah, bh, dims, preferred_element_type=F32)
        + lax.dot_general(ah, bl, dims, preferred_element_type=F32)
        + lax.dot_general(al, bh, dims, preferred_element_type=F32)
    )


RS = ("R1", "L1", "R1b", "L1b", "R2", "L2", "Z")


def kernel(
    li_hbm, og_hbm, pi_hbm, po_hbm, inv_hbm, st_hbm, len_ref, ord_ref, out_ref,
    li, og, pi, po, inv, raw, st_hi, st_lo, pg, pin, rg, rin, grads, ins, q_hi, q_lo, sc, rsc, fin,
    load_sem, gsend, grecv, rsend, rrecv, ssend, srecv, fsend, frecv,
):
    me = x, y, z, c = place()
    zlo, zhi = z % 4, z // 4
    loads = [
        pltpu.make_async_copy(src, dst, load_sem.at[n])
        for n, (src, dst) in enumerate(
            ((og_hbm, og), (po_hbm, po), (li_hbm, li), (pi_hbm, pi), (inv_hbm, inv), (st_hbm, raw.at[c]))
        )
    ]
    for copy in loads:
        copy.start()
    line = [device(x, y, zhi * 4 + (zlo + k) % 4, c) for k in (1, 2, 3)]
    partners = [
        device(x + 1, y, z, c), device(x - 1, y, z, c), device(x + 2, y, z, c),
        device(x, y + 1, z, c), device(x, y - 1, z, c), device(x, y + 2, z, c),
        device(x, y, z + 1, c), device(x, y, z - 1, c), device(x, y, z + 4, c),
        device(x, y, z, c + 1), device(x, y, z + 4, c + 1), *line,
    ]
    barrier = pltpu.get_barrier_semaphore()
    for d in partners:
        pl.semaphore_signal(barrier, inc=1, device_id=d, device_id_type=MESH)
    pl.semaphore_wait(barrier, len(partners))

    def remote(src, dst, send, recv, d):
        return pltpu.make_async_remote_copy(src, dst, send, recv, device_id=d, device_id_type=MESH)

    right, left, core = device(x + 1, y, z, c), device(x - 1, y, z, c), device(x, y, z, c + 1)
    xr, xl, xo = (x + 1) % NX, (x - 1) % NX, (x + 2) % NX
    swap = remote(st_hbm, raw.at[c], fsend.at[3], frecv.at[3], core)

    def reduce_plan(n, buf, got):
        def one(k, src, d):
            return remote(src, got.at[k], rsend.at[n, k], rrecv.at[n, k], d)

        return {
            "R1": one(0, buf.at[xo, 0], right), "L1": one(1, buf.at[xo, 1], left),
            "R1b": one(2, buf.at[xr, 1], right), "L1b": one(3, buf.at[xl, 0], left),
            "R2": one(4, buf.at[xr, 0], right), "L2": one(5, buf.at[xl, 1], left),
            "Z": one(6, buf.at[x, 1 - zhi], device(x, y, z + 4, c)),
        }

    first, second = reduce_plan(0, pg, rg), reduce_plan(1, pin, rin)

    loads[0].wait()
    loads[1].wait()
    pg[...] = jnp.dot(og[...], po[...], preferred_element_type=F32).reshape(pg.shape)
    for k in ("R1", "L1", "R1b", "L1b"):
        first[k].start()
    loads[2].wait()
    loads[3].wait()
    pin[...] = lax.dot_general(
        pi[...], li[...], (((0,), (1,)), ((), ())), preferred_element_type=F32
    ).reshape(pin.shape)
    for k in ("R1", "L1", "R1b", "L1b"):
        second[k].start()
    swap.start()

    position = lax.broadcasted_iota(jnp.int32, (8, 512), 1)
    slots, begin = jnp.zeros((8, 512), F32), jnp.int32(0)
    for k in range(QB):
        end = begin + len_ref[0, k]
        here = (position >= begin) & (position < end)
        slots = slots + jnp.where(here, ord_ref[0, k], 0).astype(F32)
        begin = end
    ins[y, zlo, 32:40, :] = slots

    def halfway(cps, buf, got):
        cps["R1"].wait_recv()
        buf[xr, 0] = buf[xr, 0] + got[0]
        cps["R2"].start()
        cps["L1"].wait_recv()
        buf[xl, 1] = buf[xl, 1] + got[1]
        cps["L2"].start()

    def reduced(cps, buf, got):
        for k in ("R1b", "L1b", "R2", "L2"):
            cps[k].wait_recv()
        buf[x, 0] = buf[x, 0] + (got[3] + got[4])
        buf[x, 1] = buf[x, 1] + (got[2] + got[5])
        cps["Z"].start()

    halfway(first, pg, rg)
    halfway(second, pin, rin)
    reduced(first, pg, rg)
    reduced(second, pin, rin)

    plan = gather_plan(me, grads, ins)
    copies = {
        m.name: remote(m.ref, m.ref, gsend.at[n], grecv.at[n], target(me, m)) for n, m in enumerate(plan)
    }
    for verb, name in order_of(plan):
        if name == "g":
            first["Z"].wait_recv()
            grads[y, zlo, x, zhi] = pg[x, zhi] + rg[6]
        elif name == "i":
            second["Z"].wait_recv()
            ins[y, zlo, 0:32, :] = pin[x, zhi] + rin[6]
        elif verb == "send":
            copies[name].start()
        else:
            copies[name].wait_recv()

    loads[4].wait()
    loads[5].wait()
    swap.wait()

    @pl.loop(0, 16)
    def _(k):
        cols = pl.ds(pl.multiple_of(k * 512, 512), 512)
        for core_of in range(2):
            high, low = split(raw[core_of, :, cols] * inv[:, cols])
            st_hi[core_of, :, cols] = high
            st_lo[core_of, :, cols] = low

    @pl.loop(0, 16)
    def _(b):
        by, bz = b // 4, b % 4
        g = split(grads[by, bz].reshape(512, 256))
        mine = ins[by, bz]
        rows = mine[0:32, :]
        member = (mine[32:33, :] == lax.broadcasted_iota(jnp.int32, (QB, 512), 0).astype(F32)).astype(F32)
        high = rows.astype(BF16).astype(F32)
        masked = [
            (v[:, None, :] * member[None]).reshape(512, 512).astype(BF16) for v in (high, rows - high)
        ]
        high, low = split(dot3(masked, g, (((1,), (0,)), ((), ()))))
        at = pl.ds(pl.multiple_of(b * QB, QB), QB)
        for i in range(32):
            q_hi[at, i * 256:(i + 1) * 256] = high[i * QB:(i + 1) * QB]
            q_lo[at, i * 256:(i + 1) * 256] = low[i * QB:(i + 1) * QB]

    sc[...] = jnp.zeros_like(sc)

    @pl.loop(0, 8)
    def _(k):
        cols = pl.ds(pl.multiple_of(k * 1024, 1024), 1024)
        q = (q_hi[:, cols], q_lo[:, cols])
        for core_of in range(2):
            part = dot3(q, (st_hi[core_of, :, cols], st_lo[core_of, :, cols]), (((1,), (1,)), ((), ())))
            sc[:, :, core_of] = sc[:, :, core_of] + part.reshape(4, 2, 32, 192)

    sends = [
        remote(sc.at[(x + hop) % NX], rsc.at[n], ssend.at[n], srecv.at[n], device(x + hop, y, z, c))
        for n, hop in enumerate((1, -1, 2))
    ]
    for copy in sends:
        copy.start()
    for copy in sends:
        copy.wait_recv()
    sc[x] = sc[x] + (rsc[0] + rsc[1]) + rsc[2]
    ends = [
        remote(sc.at[x, 1 - zhi, c], fin.at[0], fsend.at[0], frecv.at[0], device(x, y, z + 4, c)),
        remote(sc.at[x, 1 - zhi, 1 - c], fin.at[1], fsend.at[1], frecv.at[1], device(x, y, z + 4, c + 1)),
        remote(sc.at[x, zhi, 1 - c], fin.at[2], fsend.at[2], frecv.at[2], core),
    ]
    for copy in ends:
        copy.start()
    for copy in ends:
        copy.wait_recv()
    mine = sc[x, zhi, c] + fin[0]
    theirs = fin[1] + fin[2]
    for half in range(2):
        part = slice(half * QB, (half + 1) * QB)
        out_ref[pl.ds(pl.multiple_of(half * 32 + c * QB, QB), QB), :] = mine[part]
        out_ref[pl.ds(pl.multiple_of(half * 32 + (1 - c) * QB, QB), QB), :] = theirs[part]

    for copy in (*first.values(), *second.values(), *copies.values(), *sends, *ends):
        copy.wait_send()


def body(layer_input, out_grad, proj_in, proj_out, inv_diag, stored, seq_lengths, query_order):
    count = 200
    hbm, smem = pl.BlockSpec(memory_space=pl.ANY), pl.BlockSpec(memory_space=pltpu.SMEM)
    dma = pltpu.SemaphoreType.DMA
    return pl.pallas_call(
        kernel,
        out_shape=jax.ShapeDtypeStruct((64, 192), F32),
        in_specs=[hbm] * 6 + [smem] * 2,
        out_specs=pl.BlockSpec(memory_space=pltpu.VMEM),
        scratch_shapes=[
            pltpu.VMEM((512, 1024), BF16),
            pltpu.VMEM((512, 1024), BF16),
            pltpu.VMEM((1024, 256), BF16),
            pltpu.VMEM((1024, 256), BF16),
            pltpu.VMEM((1, 8192), F32),
            pltpu.VMEM((2, 192, 8192), F32),
            pltpu.VMEM((2, 192, 8192), BF16),
            pltpu.VMEM((2, 192, 8192), BF16),
            pltpu.VMEM((4, 2, 64, 256), F32),
            pltpu.VMEM((4, 2, 32, 512), F32),
            pltpu.VMEM((7, 64, 256), F32),
            pltpu.VMEM((7, 32, 512), F32),
            pltpu.VMEM((4, 4, 4, 2, TOK, 256), F32),
            pltpu.VMEM((4, 4, INROWS, 512), F32),
            pltpu.VMEM((256, 8192), BF16),
            pltpu.VMEM((256, 8192), BF16),
            pltpu.VMEM((4, 2, 2, 32, 192), F32),
            pltpu.VMEM((3, 2, 2, 32, 192), F32),
            pltpu.VMEM((3, 32, 192), F32),
            dma((6,)),
            dma((96,)), dma((96,)),
            dma((2, 7)), dma((2, 7)),
            dma((3,)), dma((3,)),
            dma((4,)), dma((4,)),
        ],
        compiler_params=pltpu.CompilerParams(
            collective_id=0, has_side_effects=True, vmem_limit_bytes=60 * 2**20
        ),
    )(layer_input, out_grad, proj_in, proj_out, inv_diag.reshape(1, -1), stored, seq_lengths, query_order)


def solution(mesh):
    return jax.shard_map(
        body,
        mesh=mesh,
        in_specs=(
            P("store", "feat"),
            P("store", "feat"),
            P("feat", None),
            P("feat", None),
            P("feat"),
            P("store", "feat"),
            P("store", None),
            P("store", None),
        ),
        out_specs=P("feat", "store"),
        check_vma=False,
    )
```

time: 419 us -> 120 us (0.29)
  waiting for transfers between devices: 373 us -> 0 us
  Pallas kernels: 0 us -> 117 us
  matrix products: 25.1 us -> 0 us
  between operations: 13.1 us -> 0.01 us
    reduce_scatter x2 -> x0, waiting for transfers between devices: 170 us -> none  [the longest x1 88.2 us: body(): lax.psum_scatter(in_terms, 'feat', scatter_dimension=1, tiled=True)]
    pallas_call x0 -> x1, Pallas kernels: none -> 117 us  [body(): pl.pallas_call(kernel, out_shape=jax.ShapeDtypeStruct((64, 192), F32), in...]
    psum x1 -> x0, waiting for transfers between devices: 103 us -> none  [body(): grad_full = lax.psum(grad_terms, 'feat')]
    all_gather x1 -> x0, waiting for transfers between devices: 99 us -> none  [body(): lax.all_gather(query_grad, 'store', axis=0, tiled=True)]
    dot_general x4 -> x0, matrix products: 25.1 us -> none  [the longest x1 18.1 us: body(): jnp.einsum('qf,rf->qr', lax.all_gather(query_grad, 'store', axis=0, tiled...]
  transfers between devices with their start and end apart: 4 -> 0, of which waited for: 4 -> 0; matrix products, arithmetic and copies ran while one was open for 1% -> 0% of each run, Pallas kernels for 0% -> 0%
where the time goes in v1:
time: 120 us; the launch traced here: 118 us
  Pallas kernels  117 us (98%)
  local copies, waits for them, and re-layouts  1.47 us (1%)
    pallas_call x1, Pallas kernels, body(): pl.pallas_call(kernel, out_shape=jax.ShapeDtypeStruct((64, 192), F32), in...  117 us

profile of v1, /device:TPU:27, one launch (start us, length us, event | category | flops | bytes accessed | tf_op | source)
XLA Modules:
  0.0 118.0 jit_solution(779598351165673202)
XLA Ops:
  0.0 116.6 %shard_map.82 = f32[64,192]{1,0:T(8,128)} custom-call(bf16[512,1024]{1,0:T(8,128)(2,1)} %li_hbm.1, bf16[512,1024]{1,0:T(8,128)(2,1)} %og_hbm.1, bf16[1024,256]{1,0:T(8,128)(2,1)} %pi_hbm.1, bf16[1024,256]{1,0:T(8,128)(2,1)} %po_hbm.1, f32[1,8192]{1,0:T(1,128)} %bitcast.1, f32[192,8192]{1,0:T(8,128)} %st_hbm.1, s32[1,16]{1,0:T(1,128)} %len_ref.1, s32[1,16]{1,0:T(1,128)} %ord_ref.1), custom_call_target="tpu_custom_call" | custom-call | tf_op jit(solution)/shard_map/pallas_call | solution.py:347
  116.6 1.5 %copy.10 = f32[64,192]{1,0:T(8,128)} copy(f32[64,192]{1,0:T(8,128)} %shard_map.82) | data formatting | bytes 98304

commit v2 on v1

--- a/solution.py
+++ b/solution.py
@@ -27,7 +27,18 @@
 
 class Message:
     def __init__(self, name, deps, kb, axis, hop, ref):
-        self.name, self.deps, self.kb, self.axis, self.hop, self.ref = name, deps, kb, axis, hop, ref
+        self.name, self.deps, self.kb, self.axis, self.hop, self.ref = name, tuple(deps), kb, axis, hop, ref
+
+
+def ring(k, sign, tag):
+    return f"{tag}{sign * k}"
+
+
+def around(tag):
+    return [ring(k, s, tag) for k in (1, 2, 3, 4) for s in (1, -1)]
+
+
+NEAR, FAR = (0, 1, -1), 2
 
 
 def gather_plan(me, grads, ins):
@@ -38,76 +49,109 @@
         return v % 4, (v % NZ) // 4
 
     def add(name, deps, kb, axis, hop, ref):
-        out.append(Message(name, tuple(deps), kb, axis, hop, ref))
-
-    def ga(zv, ys=slice(None)):
+        out.append(Message(name, deps, kb, axis, hop, ref))
+
+    def ga(zv, yv, xs=slice(None)):
         lo, hi = zz(zv)
-        return grads.at[ys, lo, :, hi, A0:B0, :]
-
-    def gb(zv, xv, ys=slice(None)):
+        return grads.at[yv % NY, lo, xs, hi, A0:B0, :]
+
+    def gb(zv, yv, xv):
         lo, hi = zz(zv)
-        return grads.at[ys, lo, xv % NX, hi, B0:C0, :]
-
-    def gc(xv, yv, zs=slice(None)):
-        return grads.at[yv % NY, zs, xv % NX, :, C0:TOK, :]
+        return grads.at[yv % NY, lo, xv % NX, hi, B0:C0, :]
+
+    def gz(xv, yv, rows, zs=slice(None)):
+        return grads.at[yv % NY, zs, xv % NX, :, rows, :]
 
     first, second = pl.ds(0, 2), pl.ds(2, 2)
+    brows, crows = slice(B0, C0), slice(C0, TOK)
+    ka, kb, kc = (B0 - A0), (C0 - B0), (TOK - C0)
     lo, hi = zz(z)
+    from_y = {1: -1, -1: 1, 2: 2}
     for k in (1, 2, 3, 4):
         for sign in (1, -1):
             zlo, zhi = zz(z - sign * (k - 1))
             cols = slice(None) if k < 4 else pl.ds(0 if sign > 0 else 128, 128)
-            deps = ["g"] if k == 1 else [f"Cz{sign * (k - 1)}"]
-            add(f"Cz{sign * k}", deps, 24 if k < 4 else 12, "z", sign, grads.at[y, zlo, x, zhi, C0:TOK, cols])
-    call = [f"Cz{s * k}" for k in (1, 2, 3, 4) for s in (1, -1)]
-    for sign in (1, -1):
-        add(f"Cx{sign}", ["g"] + call, 192, "x", sign, gc(x, y))
-    for sign in (1, -1):
-        add(f"Cx{2 * sign}", [f"Cx{sign}"], 96, "x", sign, gc(x - sign, y, first if sign > 0 else second))
+            deps = ["g"] if k == 1 else [ring(k - 1, sign, "Cz")]
+            add(ring(k, sign, "Cz"), deps, kc if k < 4 else kc / 2, "z", sign, grads.at[y, zlo, x, zhi, crows, cols])
+    call = ["g"] + around("Cz")
     for hop in (1, -1, 2):
-        add(f"By{hop}", ["g"], 24, "y", hop, grads.at[y, lo, x, hi, B0:C0, :])
-    ball = ["g"] + [f"By{h}" for h in (1, -1, 2)]
-    for k in (1, 2, 3, 4):
-        for sign in (1, -1):
-            deps = ball if k == 1 else [f"Bz{sign * (k - 1)}"]
-            ys = slice(None) if k < 4 else (first if sign > 0 else second)
-            add(f"Bz{sign * k}", deps, 96 if k < 4 else 48, "z", sign, gb(z - sign * (k - 1), x, ys))
-    for hop in (1, -1, 2):
-        add(f"Ax{hop}", ["g"], 16, "x", hop, grads.at[y, lo, x, hi, A0:B0, :])
+        add(f"Ax{hop}", ["g"], ka, "x", hop, grads.at[y, lo, x, hi, A0:B0, :])
     aall = ["g"] + [f"Ax{h}" for h in (1, -1, 2)]
     for hop in (1, -1, 2):
-        add(f"Ay{hop}", aall, 64, "y", hop, grads.at[y, lo, :, hi, A0:B0, :])
+        add(f"By{hop}", ["g"], kb, "y", hop, gb(z, y, x))
+    for hop in (1, -1, 2):
+        add(f"Ay{hop}", aall, 4 * ka, "y", hop, ga(z, y))
+    for sign in (1, -1):
+        add(f"Cx{sign}", call, 8 * kc, "x", sign, gz(x, y, crows))
+    for sign in (1, -1):
+        half = first if sign > 0 else second
+        add(f"Cx{2 * sign}", [f"Cx{sign}"], 4 * kc, "x", sign, gz(x - sign, y, crows, half))
     for k in (1, 2, 3):
-        add(f"Iz{k}", ["i"], 80, "i", k, ins.at[y, lo])
+        add(f"Iz{k}", ["i", "Cz3", "Cz-3"], 80, "i", k, ins.at[y, lo])
     iall = ["i"] + [f"Iz{k}" for k in (1, 2, 3)]
-    for sign in (1, -1):
-        add(f"Iy{sign}", iall, 320, "y", sign, ins.at[y])
-    for sign in (1, -1):
-        add(f"Iy{2 * sign}", [f"Iy{sign}"], 160, "y", sign, ins.at[(y - sign) % NY, first if sign > 0 else second])
-    for d in (0, -1, 1, -2, 2, -3, 3, 4):
-        if d == 0:
-            deps = ball
-        elif d == 4:
-            deps = ["Bz4", "Bz-4"]
+    needs = {}
+    for r in (*NEAR, FAR):
+        tag = f"B{r}z"
+        here = ["g"] if r == 0 else [f"By{from_y[r]}"]
+        held = ["A0z2", "A0z-2"] if r == FAR else []
+        for k in (1, 2, 3, 4):
+            for sign in (1, -1):
+                deps = here + held if k == 1 else [ring(k - 1, sign, tag)]
+                zv = z - sign * (k - 1)
+                ref = gb(zv, y + r, x)
+                if k == 4:
+                    zlo, zhi = zz(zv)
+                    ref = grads.at[(y + r) % NY, zlo, x, zhi, brows, pl.ds(0 if sign > 0 else 128, 128)]
+                add(ring(k, sign, tag), deps, kb if k < 4 else kb / 2, "z", sign, ref)
+        ball = here + around(tag)
+        brought = []
+        if r == 0:
+            for d in (0, -1, 1, -2, 2, -3, 3, 4):
+                deps = ["g"] if d == 0 else ([ring(4, 1, tag), ring(4, -1, tag)] if d == 4 else [f"{tag}{-d}"])
+                for sign in (1, -1):
+                    add(f"B0x{sign},{d}", deps, kb, "x", sign, gb(z + d, y, x))
+            came = {s: [f"B0x{s},{d}" for d in (0, -1, 1, -2, 2, -3, 3, 4)] for s in (1, -1)}
         else:
-            deps = [f"Bz{-d}"]
+            for sign in (1, -1):
+                add(f"B{r}x{sign}", ball + (["B1x1", "B1x-1"] if r == FAR else []), 8 * kb, "x", sign, gz(x, y + r, brows))
+            came = {s: [f"B{r}x{s}"] for s in (1, -1)}
         for sign in (1, -1):
-            add(f"Bx{d},{sign}", deps, 96, "x", sign, gb(z + d, x))
-        for sign in (1, -1):
-            add(f"Bx{d},{2 * sign}", [f"Bx{d},{sign}"], 48, "x", sign, gb(z + d, x - sign, first if sign > 0 else second))
-    for d in (0, -1, 1, 2):
-        deps = (["g"] + call) if d == 0 else (["Cx2", "Cx-2"] if d == 2 else [f"Cx{-d}"])
-        for sign in (1, -1):
-            add(f"Cy{d},{sign}", deps, 192, "y", sign, gc(x + d, y))
-        for sign in (1, -1):
-            add(f"Cy{d},{2 * sign}", [f"Cy{d},{sign}"], 96, "y", sign, gc(x + d, y - sign, first if sign > 0 else second))
-    yall = aall + [f"Ay{h}" for h in (1, -1, 2)]
-    for k in (1, 2, 3, 4):
-        for sign in (1, -1):
-            deps = yall if k == 1 else [f"Az{sign * (k - 1)}"]
-            ys = slice(None) if k < 4 else (first if sign > 0 else second)
-            add(f"Az{sign * k}", deps, 256 if k < 4 else 128, "z", sign, ga(z - sign * (k - 1), ys))
-    return out
+            half = first if sign > 0 else second
+            add(f"B{r}x{2 * sign}", came[sign], 4 * kb, "x", sign, gz(x - sign, y + r, brows, half))
+            brought += came[sign] + [f"B{r}x{2 * sign}"]
+        tag = f"A{r}z"
+        here = aall if r == 0 else [f"Ay{from_y[r]}"]
+        held = ["A1z3", "A-1z3"] if r == FAR else ["B1z3", "B1z-3"]
+        for k in (1, 2, 3, 4):
+            for sign in (1, -1):
+                deps = here + held if k == 1 else [ring(k - 1, sign, tag)]
+                xs = slice(None) if k < 4 else (first if sign > 0 else second)
+                ref = ga(z - sign * (k - 1), y + r, xs)
+                add(ring(k, sign, tag), deps, 4 * ka if k < 4 else 2 * ka, "z", sign, ref)
+        needs[r] = ball + brought + here + around(tag)
+        if r == 0:
+            needs[r] += call + ["Cx1", "Cx-1", "Cx2", "Cx-2"] + iall
+            for d in (0, -1, 1, 2):
+                deps = call if d == 0 else (["Cx2", "Cx-2"] if d == 2 else [f"Cx{-d}"])
+                for sign in (1, -1):
+                    add(f"C{d}y{sign}", deps, 8 * kc, "y", sign, gz(x + d, y, crows))
+            for sign in (1, -1):
+                add(f"Iy{sign}", iall, 320, "y", sign, ins.at[y])
+        elif r != FAR:
+            sign = from_y[r]
+            needs[r] += [f"C{d}y{sign}" for d in (0, -1, 1, 2)] + [f"Iy{sign}"]
+        else:
+            for sign in (1, -1):
+                half = first if sign > 0 else second
+                add(f"Iy{2 * sign}", [f"Iy{sign}", f"C2y{sign}"], 160, "y", sign, ins.at[(y - sign) % NY, half])
+                needs[r] += [f"Iy{2 * sign}"]
+            for d in (0, -1, 1, 2):
+                for sign in (1, -1):
+                    half = first if sign > 0 else second
+                    deps = [f"C{d}y{sign}", f"C1y{sign}"]
+                    add(f"C{d}y{2 * sign}", deps, 4 * kc, "y", sign, gz(x + d, y - sign, crows, half))
+                    needs[r] += [f"C{d}y{2 * sign}"]
+    return out, needs
 
 
 def target(me, m):
@@ -121,13 +165,20 @@
     return device(x, y, (z // 4) * 4 + (z % 4 + m.hop) % 4, c)
 
 
-def order_of(plan, late=8.0):
-    rate, latency = 42.0, 1.5
+def order_of(plan, tasks, rate=38.0, latency=2.0, late=4.0):
     free, got, sent, events, steps = {}, set(), set(), [(0.0, 0, "g"), (late, 1, "i")], []
     heapq.heapify(events)
-    count = 2
-    while events:
-        now, _, name = heapq.heappop(events)
+    count, now, todo, idle = 2, 0.0, list(tasks), 0.0
+    while events or todo:
+        ready = next((t for t in todo if all(d in got for d in t[1])), None)
+        if ready and not (events and events[0][0] <= now):
+            todo.remove(ready)
+            steps.append(("task", ready[0]))
+            got.add(ready[0])
+            now += ready[2]
+            continue
+        at, _, name = heapq.heappop(events)
+        now = max(now, at)
         got.add(name)
         steps.append(("wait", name))
         for m in plan:
@@ -146,7 +197,7 @@
                 free[k] = end
             heapq.heappush(events, (end + latency, count, m.name))
             count += 1
-    return steps
+    return steps, now
 
 
 def split(v):
@@ -168,7 +219,7 @@
 
 def kernel(
     li_hbm, og_hbm, pi_hbm, po_hbm, inv_hbm, st_hbm, len_ref, ord_ref, out_ref,
-    li, og, pi, po, inv, raw, st_hi, st_lo, pg, pin, rg, rin, grads, ins, q_hi, q_lo, sc, rsc, fin,
+    li, og, pi, po, inv, raw, st_hi, st_lo, pg, pin, rg, rin, grads, ins, q, sc, rsc, fin,
     load_sem, gsend, grecv, rsend, rrecv, ssend, srecv, fsend, frecv,
 ):
     me = x, y, z, c = place()
@@ -179,7 +230,7 @@
             ((og_hbm, og), (po_hbm, po), (li_hbm, li), (pi_hbm, pi), (inv_hbm, inv), (st_hbm, raw.at[c]))
         )
     ]
-    for copy in loads:
+    for copy in loads[:5]:
         copy.start()
     line = [device(x, y, zhi * 4 + (zlo + k) % 4, c) for k in (1, 2, 3)]
     partners = [
@@ -225,6 +276,7 @@
     ).reshape(pin.shape)
     for k in ("R1", "L1", "R1b", "L1b"):
         second[k].start()
+    loads[5].start()
     swap.start()
 
     position = lax.broadcasted_iota(jnp.int32, (8, 512), 1)
@@ -256,11 +308,108 @@
     reduced(first, pg, rg)
     reduced(second, pin, rin)
 
-    plan = gather_plan(me, grads, ins)
+    plan, needs = gather_plan(me, grads, ins)
     copies = {
         m.name: remote(m.ref, m.ref, gsend.at[n], grecv.at[n], target(me, m)) for n, m in enumerate(plan)
     }
-    for verb, name in order_of(plan):
+
+    def prepare(part):
+        if part == 0:
+            loads[4].wait()
+            loads[5].wait()
+            swap.wait()
+
+        @pl.loop(part * 4, part * 4 + 4)
+        def _(k):
+            cols = pl.ds(pl.multiple_of(k * 512, 512), 512)
+            for core_of in range(2):
+                high, low = split(raw[core_of, :, cols] * inv[:, cols])
+                st_hi[core_of, :, cols] = high
+                st_lo[core_of, :, cols] = low
+
+    def outer(r, part):
+        by = (y + r) % NY
+        high_at = NEAR.index(r) * 64 if r != FAR else 384
+        low_at = high_at + (192 if r != FAR else 64)
+
+        @pl.loop(part * 2, part * 2 + 2)
+        def _(bz):
+            g = split(grads[by, bz].reshape(512, 256))
+            mine = ins[by, bz]
+            rows = mine[0:32, :]
+            member = (mine[32:33, :] == lax.broadcasted_iota(jnp.int32, (QB, 512), 0).astype(F32)).astype(F32)
+            high = rows.astype(BF16).astype(F32)
+            masked = [
+                (v[:, None, :] * member[None]).reshape(512, 512).astype(BF16) for v in (high, rows - high)
+            ]
+            high, low = split(dot3(masked, g, (((1,), (0,)), ((), ()))))
+            for i in range(32):
+                cols = slice(i * 256, (i + 1) * 256)
+                q[pl.ds(pl.multiple_of(high_at + bz * QB, QB), QB), cols] = high[i * QB:(i + 1) * QB]
+                q[pl.ds(pl.multiple_of(low_at + bz * QB, QB), QB), cols] = low[i * QB:(i + 1) * QB]
+
+    last = (((1,), (1,)), ((), ()))
+
+    def near_scores(part):
+        if part == 0:
+            sc[...] = jnp.zeros_like(sc)
+
+        @pl.loop(part * 2, part * 2 + 2)
+        def _(k):
+            cols = pl.ds(pl.multiple_of(k * 1024, 1024), 1024)
+            for core_of in range(2):
+                both = lax.dot_general(q[0:384, cols], st_hi[core_of, :, cols], last, preferred_element_type=F32)
+                high = lax.dot_general(q[0:192, cols], st_lo[core_of, :, cols], last, preferred_element_type=F32)
+                total = both[0:192] + both[192:384] + high
+                for n, r in enumerate(NEAR):
+                    to = (y + r) % NX
+                    sc[to, :, core_of] = sc[to, :, core_of] + total[n * 64:(n + 1) * 64].reshape(2, 32, 192)
+
+    def far_scores():
+        def step(k, total):
+            cols = pl.ds(pl.multiple_of(k * 1024, 1024), 1024)
+            sums = []
+            for core_of in range(2):
+                both = lax.dot_general(st_hi[core_of, :, cols], q[384:512, cols], last, preferred_element_type=F32)
+                high = lax.dot_general(st_lo[core_of, :, cols], q[384:448, cols], last, preferred_element_type=F32)
+                sums.append((total[core_of][0] + both, total[core_of][1] + high))
+            return tuple(sums)
+
+        zero = (jnp.zeros((192, 128), F32), jnp.zeros((192, 64), F32))
+        total = lax.fori_loop(0, 8, step, (zero, zero))
+        for core_of in range(2):
+            both, high = total[core_of]
+            rows = (both[:, 0:64] + both[:, 64:128] + high).T
+            sc[(y + FAR) % NX, :, core_of] = rows.reshape(2, 32, 192)
+
+    def pass_on(r):
+        to = (y + r) % NX
+        slot = (x - to + NX - 1) % NX
+
+        @pl.when(to != x)
+        def _():
+            remote(sc.at[to], rsc.at[slot], ssend.at[slot], srecv.at[slot], device(to, y, z, c)).start()
+
+    tasks = [(f"prepare{n}", (), 0.6) for n in range(4)]
+    run = {f"prepare{n}": (prepare, (n,)) for n in range(4)}
+    done = [f"prepare{n}" for n in range(4)]
+    for r in NEAR:
+        for n in range(2):
+            tasks.append((f"outer{r},{n}", tuple(needs[r]), 1.3))
+            run[f"outer{r},{n}"] = (outer, (r, n))
+            done.append(f"outer{r},{n}")
+    for n in range(4):
+        tasks.append((f"near{n}", tuple(done), 1.5))
+        run[f"near{n}"] = (near_scores, (n,))
+        done.append(f"near{n}")
+    for r in NEAR:
+        tasks.append((f"pass{r}", tuple(done), 0.1))
+        run[f"pass{r}"] = (pass_on, (r,))
+    for n in range(2):
+        tasks.append((f"outer{FAR},{n}", tuple(done) + tuple(needs[FAR]), 1.3))
+        run[f"outer{FAR},{n}"] = (outer, (FAR, n))
+
+    for verb, name in order_of(plan, tasks)[0]:
         if name == "g":
             first["Z"].wait_recv()
             grads[y, zlo, x, zhi] = pg[x, zhi] + rg[6]
@@ -269,54 +418,17 @@
             ins[y, zlo, 0:32, :] = pin[x, zhi] + rin[6]
         elif verb == "send":
             copies[name].start()
+        elif verb == "wait":
+            copies[name].wait_recv()
         else:
-            copies[name].wait_recv()
-
-    loads[4].wait()
-    loads[5].wait()
-    swap.wait()
-
-    @pl.loop(0, 16)
-    def _(k):
-        cols = pl.ds(pl.multiple_of(k * 512, 512), 512)
-        for core_of in range(2):
-            high, low = split(raw[core_of, :, cols] * inv[:, cols])
-            st_hi[core_of, :, cols] = high
-            st_lo[core_of, :, cols] = low
-
-    @pl.loop(0, 16)
-    def _(b):
-        by, bz = b // 4, b % 4
-        g = split(grads[by, bz].reshape(512, 256))
-        mine = ins[by, bz]
-        rows = mine[0:32, :]
-        member = (mine[32:33, :] == lax.broadcasted_iota(jnp.int32, (QB, 512), 0).astype(F32)).astype(F32)
-        high = rows.astype(BF16).astype(F32)
-        masked = [
-            (v[:, None, :] * member[None]).reshape(512, 512).astype(BF16) for v in (high, rows - high)
-        ]
-        high, low = split(dot3(masked, g, (((1,), (0,)), ((), ()))))
-        at = pl.ds(pl.multiple_of(b * QB, QB), QB)
-        for i in range(32):
-            q_hi[at, i * 256:(i + 1) * 256] = high[i * QB:(i + 1) * QB]
-            q_lo[at, i * 256:(i + 1) * 256] = low[i * QB:(i + 1) * QB]
-
-    sc[...] = jnp.zeros_like(sc)
-
-    @pl.loop(0, 8)
-    def _(k):
-        cols = pl.ds(pl.multiple_of(k * 1024, 1024), 1024)
-        q = (q_hi[:, cols], q_lo[:, cols])
-        for core_of in range(2):
-            part = dot3(q, (st_hi[core_of, :, cols], st_lo[core_of, :, cols]), (((1,), (1,)), ((), ())))
-            sc[:, :, core_of] = sc[:, :, core_of] + part.reshape(4, 2, 32, 192)
+            work, given = run[name]
+            work(*given)
+    far_scores()
+    pass_on(FAR)
 
     sends = [
-        remote(sc.at[(x + hop) % NX], rsc.at[n], ssend.at[n], srecv.at[n], device(x + hop, y, z, c))
-        for n, hop in enumerate((1, -1, 2))
+        remote(sc.at[x], rsc.at[n], ssend.at[n], srecv.at[n], right) for n in range(3)
     ]
-    for copy in sends:
-        copy.start()
     for copy in sends:
         copy.wait_recv()
     sc[x] = sc[x] + (rsc[0] + rsc[1]) + rsc[2]
@@ -341,7 +453,6 @@
 
 
 def body(layer_input, out_grad, proj_in, proj_out, inv_diag, stored, seq_lengths, query_order):
-    count = 200
     hbm, smem = pl.BlockSpec(memory_space=pl.ANY), pl.BlockSpec(memory_space=pltpu.SMEM)
     dma = pltpu.SemaphoreType.DMA
     return pl.pallas_call(
@@ -364,13 +475,12 @@
             pltpu.VMEM((7, 32, 512), F32),
             pltpu.VMEM((4, 4, 4, 2, TOK, 256), F32),
             pltpu.VMEM((4, 4, INROWS, 512), F32),
-            pltpu.VMEM((256, 8192), BF16),
-            pltpu.VMEM((256, 8192), BF16),
+            pltpu.VMEM((512, 8192), BF16),
             pltpu.VMEM((4, 2, 2, 32, 192), F32),
             pltpu.VMEM((3, 2, 2, 32, 192), F32),
             pltpu.VMEM((3, 32, 192), F32),
             dma((6,)),
-            dma((96,)), dma((96,)),
+            dma((160,)), dma((160,)),
             dma((2, 7)), dma((2, 7)),
             dma((3,)), dma((3,)),
             dma((4,)), dma((4,)),

time: 120 us -> 110 us (0.917); the launches traced: 118 us -> 109 us
  Pallas kernels: 117 us -> 108 us
    pallas_call x1, Pallas kernels: 117 us -> 108 us  [body(): pl.pallas_call(kernel, out_shape=jax.ShapeDtypeStruct((64, 192), F32), in...]
where the time goes in v2:
time: 110 us; the launch traced here: 109 us
  Pallas kernels  108 us (98%)
  local copies, waits for them, and re-layouts  1.47 us (1%)
    pallas_call x1, Pallas kernels, body(): pl.pallas_call(kernel, out_shape=jax.ShapeDtypeStruct((64, 192), F32), in...  108 us

profile of v2, /device:TPU:27, one launch (start us, length us, event | category | flops | bytes accessed | tf_op | source)
XLA Modules:
  0.0 109.4 jit_solution(8884621387862758446)
XLA Ops:
  0.0 107.9 %shard_map.82 = f32[64,192]{1,0:T(8,128)} custom-call(bf16[512,1024]{1,0:T(8,128)(2,1)} %li_hbm.1, bf16[512,1024]{1,0:T(8,128)(2,1)} %og_hbm.1, bf16[1024,256]{1,0:T(8,128)(2,1)} %pi_hbm.1, bf16[1024,256]{1,0:T(8,128)(2,1)} %po_hbm.1, f32[1,8192]{1,0:T(1,128)} %bitcast.1, f32[192,8192]{1,0:T(8,128)} %st_hbm.1, s32[1,16]{1,0:T(1,128)} %len_ref.1, s32[1,16]{1,0:T(1,128)} %ord_ref.1), custom_call_target="tpu_custom_call" | custom-call | tf_op jit(solution)/shard_map/pallas_call | solution.py:458
  108.0 1.5 %copy.10 = f32[64,192]{1,0:T(8,128)} copy(f32[64,192]{1,0:T(8,128)} %shard_map.82) | data formatting | bytes 98304

commit v3 on v2

--- a/solution.py
+++ b/solution.py
@@ -12,7 +12,7 @@
 NX, NY, NZ = 4, 4, 8
 QB = 16
 A0, B0, C0, TOK = 0, 16, 40, 64
-INROWS = 40
+INROWS = 136
 
 
 def place():
@@ -87,13 +87,14 @@
         half = first if sign > 0 else second
         add(f"Cx{2 * sign}", [f"Cx{sign}"], 4 * kc, "x", sign, gz(x - sign, y, crows, half))
     for k in (1, 2, 3):
-        add(f"Iz{k}", ["i", "Cz3", "Cz-3"], 80, "i", k, ins.at[y, lo])
+        add(f"Iz{k}", ["i", "Cz3", "Cz-3"], 68, "i", k, ins.at[y, lo])
     iall = ["i"] + [f"Iz{k}" for k in (1, 2, 3)]
     needs = {}
+    across = {s: [f"C0y{s},{d}" for d in (0, -1, 1, -2, 2, -3, 3, 4)] for s in (1, -1)}
     for r in (*NEAR, FAR):
         tag = f"B{r}z"
         here = ["g"] if r == 0 else [f"By{from_y[r]}"]
-        held = ["A0z2", "A0z-2"] if r == FAR else []
+        held = ["A0z1", "A0z-1"] if r == FAR else []
         for k in (1, 2, 3, 4):
             for sign in (1, -1):
                 deps = here + held if k == 1 else [ring(k - 1, sign, tag)]
@@ -131,24 +132,29 @@
         needs[r] = ball + brought + here + around(tag)
         if r == 0:
             needs[r] += call + ["Cx1", "Cx-1", "Cx2", "Cx-2"] + iall
-            for d in (0, -1, 1, 2):
-                deps = call if d == 0 else (["Cx2", "Cx-2"] if d == 2 else [f"Cx{-d}"])
+            for d in (0, -1, 1, -2, 2, -3, 3, 4):
+                deps = ["g"] if d == 0 else (["Cz4", "Cz-4"] if d == 4 else [f"Cz{-d}"])
+                zlo, zhi = zz(z + d)
+                for sign in (1, -1):
+                    add(f"C0y{sign},{d}", deps, kc, "y", sign, grads.at[y, zlo, x, zhi, crows, :])
+            for d in (-1, 1, 2):
+                deps = ["Cx2", "Cx-2"] if d == 2 else [f"Cx{-d}"]
                 for sign in (1, -1):
                     add(f"C{d}y{sign}", deps, 8 * kc, "y", sign, gz(x + d, y, crows))
             for sign in (1, -1):
-                add(f"Iy{sign}", iall, 320, "y", sign, ins.at[y])
+                add(f"Iy{sign}", iall, 272, "y", sign, ins.at[y])
         elif r != FAR:
             sign = from_y[r]
-            needs[r] += [f"C{d}y{sign}" for d in (0, -1, 1, 2)] + [f"Iy{sign}"]
+            needs[r] += [f"C{d}y{sign}" for d in (-1, 1, 2)] + across[sign] + [f"Iy{sign}"]
         else:
             for sign in (1, -1):
                 half = first if sign > 0 else second
-                add(f"Iy{2 * sign}", [f"Iy{sign}", f"C2y{sign}"], 160, "y", sign, ins.at[(y - sign) % NY, half])
+                add(f"Iy{2 * sign}", [f"Iy{sign}", f"C2y{sign}"], 136, "y", sign, ins.at[(y - sign) % NY, half])
                 needs[r] += [f"Iy{2 * sign}"]
             for d in (0, -1, 1, 2):
                 for sign in (1, -1):
                     half = first if sign > 0 else second
-                    deps = [f"C{d}y{sign}", f"C1y{sign}"]
+                    deps = (across[sign] if d == 0 else [f"C{d}y{sign}"]) + [f"C1y{sign}"]
                     add(f"C{d}y{2 * sign}", deps, 4 * kc, "y", sign, gz(x + d, y - sign, crows, half))
                     needs[r] += [f"C{d}y{2 * sign}"]
     return out, needs
@@ -224,10 +230,11 @@
 ):
     me = x, y, z, c = place()
     zlo, zhi = z % 4, z // 4
+    rows_of = pl.ds(pl.multiple_of(c * 192, 192), 192)
     loads = [
         pltpu.make_async_copy(src, dst, load_sem.at[n])
         for n, (src, dst) in enumerate(
-            ((og_hbm, og), (po_hbm, po), (li_hbm, li), (pi_hbm, pi), (inv_hbm, inv), (st_hbm, raw.at[c]))
+            ((og_hbm, og), (po_hbm, po), (li_hbm, li), (pi_hbm, pi), (inv_hbm, inv), (st_hbm, raw.at[rows_of]))
         )
     ]
     for copy in loads[:5]:
@@ -242,14 +249,13 @@
     barrier = pltpu.get_barrier_semaphore()
     for d in partners:
         pl.semaphore_signal(barrier, inc=1, device_id=d, device_id_type=MESH)
-    pl.semaphore_wait(barrier, len(partners))
 
     def remote(src, dst, send, recv, d):
         return pltpu.make_async_remote_copy(src, dst, send, recv, device_id=d, device_id_type=MESH)
 
     right, left, core = device(x + 1, y, z, c), device(x - 1, y, z, c), device(x, y, z, c + 1)
     xr, xl, xo = (x + 1) % NX, (x - 1) % NX, (x + 2) % NX
-    swap = remote(st_hbm, raw.at[c], fsend.at[3], frecv.at[3], core)
+    swap = remote(st_hbm, raw.at[rows_of], fsend.at[3], frecv.at[3], core)
 
     def reduce_plan(n, buf, got):
         def one(k, src, d):
@@ -267,6 +273,7 @@
     loads[0].wait()
     loads[1].wait()
     pg[...] = jnp.dot(og[...], po[...], preferred_element_type=F32).reshape(pg.shape)
+    pl.semaphore_wait(barrier, len(partners))
     for k in ("R1", "L1", "R1b", "L1b"):
         first[k].start()
     loads[2].wait()
@@ -279,14 +286,14 @@
     loads[5].start()
     swap.start()
 
-    position = lax.broadcasted_iota(jnp.int32, (8, 512), 1)
-    slots, begin = jnp.zeros((8, 512), F32), jnp.int32(0)
+    position = lax.broadcasted_iota(jnp.int32, (8, 128), 0) * 128 + lax.broadcasted_iota(jnp.int32, (8, 128), 1)
+    slots, begin = jnp.zeros((8, 128), F32), jnp.int32(0)
     for k in range(QB):
         end = begin + len_ref[0, k]
         here = (position >= begin) & (position < end)
         slots = slots + jnp.where(here, ord_ref[0, k], 0).astype(F32)
         begin = end
-    ins[y, zlo, 32:40, :] = slots
+    ins[y, zlo, 128:136, :] = slots
 
     def halfway(cps, buf, got):
         cps["R1"].wait_recv()
@@ -322,10 +329,9 @@
         @pl.loop(part * 4, part * 4 + 4)
         def _(k):
             cols = pl.ds(pl.multiple_of(k * 512, 512), 512)
-            for core_of in range(2):
-                high, low = split(raw[core_of, :, cols] * inv[:, cols])
-                st_hi[core_of, :, cols] = high
-                st_lo[core_of, :, cols] = low
+            high, low = split(raw[:, cols] * inv[:, cols])
+            st_hi[:, cols] = high
+            st_lo[:, cols] = low
 
     def outer(r, part):
         by = (y + r) % NY
@@ -336,8 +342,9 @@
         def _(bz):
             g = split(grads[by, bz].reshape(512, 256))
             mine = ins[by, bz]
-            rows = mine[0:32, :]
-            member = (mine[32:33, :] == lax.broadcasted_iota(jnp.int32, (QB, 512), 0).astype(F32)).astype(F32)
+            rows = jnp.concatenate([mine[32 * k:32 * k + 32] for k in range(4)], axis=1)
+            slot = jnp.concatenate([mine[128 + k:129 + k] for k in range(4)], axis=1)
+            member = (slot == lax.broadcasted_iota(jnp.int32, (QB, 512), 0).astype(F32)).astype(F32)
             high = rows.astype(BF16).astype(F32)
             masked = [
                 (v[:, None, :] * member[None]).reshape(512, 512).astype(BF16) for v in (high, rows - high)
@@ -357,30 +364,23 @@
         @pl.loop(part * 2, part * 2 + 2)
         def _(k):
             cols = pl.ds(pl.multiple_of(k * 1024, 1024), 1024)
-            for core_of in range(2):
-                both = lax.dot_general(q[0:384, cols], st_hi[core_of, :, cols], last, preferred_element_type=F32)
-                high = lax.dot_general(q[0:192, cols], st_lo[core_of, :, cols], last, preferred_element_type=F32)
-                total = both[0:192] + both[192:384] + high
-                for n, r in enumerate(NEAR):
-                    to = (y + r) % NX
-                    sc[to, :, core_of] = sc[to, :, core_of] + total[n * 64:(n + 1) * 64].reshape(2, 32, 192)
+            both = lax.dot_general(q[0:384, cols], st_hi[:, cols], last, preferred_element_type=F32)
+            high = lax.dot_general(q[0:192, cols], st_lo[:, cols], last, preferred_element_type=F32)
+            total = both[0:192] + both[192:384] + high
+            for n, r in enumerate(NEAR):
+                to = (y + r) % NX
+                sc[to] = sc[to] + total[n * 64:(n + 1) * 64].reshape(2, 32, 384)
 
     def far_scores():
         def step(k, total):
             cols = pl.ds(pl.multiple_of(k * 1024, 1024), 1024)
-            sums = []
-            for core_of in range(2):
-                both = lax.dot_general(st_hi[core_of, :, cols], q[384:512, cols], last, preferred_element_type=F32)
-                high = lax.dot_general(st_lo[core_of, :, cols], q[384:448, cols], last, preferred_element_type=F32)
-                sums.append((total[core_of][0] + both, total[core_of][1] + high))
-            return tuple(sums)
-
-        zero = (jnp.zeros((192, 128), F32), jnp.zeros((192, 64), F32))
-        total = lax.fori_loop(0, 8, step, (zero, zero))
-        for core_of in range(2):
-            both, high = total[core_of]
-            rows = (both[:, 0:64] + both[:, 64:128] + high).T
-            sc[(y + FAR) % NX, :, core_of] = rows.reshape(2, 32, 192)
+            both = lax.dot_general(st_hi[:, cols], q[384:512, cols], last, preferred_element_type=F32)
+            high = lax.dot_general(st_lo[:, cols], q[384:448, cols], last, preferred_element_type=F32)
+            return total[0] + both, total[1] + high
+
+        both, high = lax.fori_loop(0, 8, step, (jnp.zeros((384, 128), F32), jnp.zeros((384, 64), F32)))
+        rows = (both[:, 0:64] + both[:, 64:128] + high).T
+        sc[(y + FAR) % NX] = rows.reshape(2, 32, 384)
 
     def pass_on(r):
         to = (y + r) % NX
@@ -415,7 +415,9 @@
             grads[y, zlo, x, zhi] = pg[x, zhi] + rg[6]
         elif name == "i":
             second["Z"].wait_recv()
-            ins[y, zlo, 0:32, :] = pin[x, zhi] + rin[6]
+            whole = pin[x, zhi] + rin[6]
+            for k in range(4):
+                ins[y, zlo, 32 * k:32 * k + 32, :] = whole[:, 128 * k:128 * k + 128]
         elif verb == "send":
             copies[name].start()
         elif verb == "wait":
@@ -432,17 +434,20 @@
     for copy in sends:
         copy.wait_recv()
     sc[x] = sc[x] + (rsc[0] + rsc[1]) + rsc[2]
+    ours, others = (pl.ds(pl.multiple_of(k * 128, 128), 256) for k in (c, 1 - c))
     ends = [
-        remote(sc.at[x, 1 - zhi, c], fin.at[0], fsend.at[0], frecv.at[0], device(x, y, z + 4, c)),
-        remote(sc.at[x, 1 - zhi, 1 - c], fin.at[1], fsend.at[1], frecv.at[1], device(x, y, z + 4, c + 1)),
-        remote(sc.at[x, zhi, 1 - c], fin.at[2], fsend.at[2], frecv.at[2], core),
+        remote(sc.at[x, 1 - zhi, :, ours], fin.at[0], fsend.at[0], frecv.at[0], device(x, y, z + 4, c)),
+        remote(sc.at[x, 1 - zhi, :, others], fin.at[1], fsend.at[1], frecv.at[1], device(x, y, z + 4, c + 1)),
+        remote(sc.at[x, zhi, :, others], fin.at[2], fsend.at[2], frecv.at[2], core),
     ]
     for copy in ends:
         copy.start()
     for copy in ends:
         copy.wait_recv()
-    mine = sc[x, zhi, c] + fin[0]
-    theirs = fin[1] + fin[2]
+    mine, theirs = (
+        jnp.where(c == 0, v[:, 0:192], v[:, 64:256])
+        for v in (sc[x, zhi, :, ours] + fin[0], fin[1] + fin[2])
+    )
     for half in range(2):
         part = slice(half * QB, (half + 1) * QB)
         out_ref[pl.ds(pl.multiple_of(half * 32 + c * QB, QB), QB), :] = mine[part]
@@ -466,19 +471,19 @@
             pltpu.VMEM((1024, 256), BF16),
             pltpu.VMEM((1024, 256), BF16),
             pltpu.VMEM((1, 8192), F32),
-            pltpu.VMEM((2, 192, 8192), F32),
-            pltpu.VMEM((2, 192, 8192), BF16),
-            pltpu.VMEM((2, 192, 8192), BF16),
+            pltpu.VMEM((384, 8192), F32),
+            pltpu.VMEM((384, 8192), BF16),
+            pltpu.VMEM((384, 8192), BF16),
             pltpu.VMEM((4, 2, 64, 256), F32),
             pltpu.VMEM((4, 2, 32, 512), F32),
             pltpu.VMEM((7, 64, 256), F32),
             pltpu.VMEM((7, 32, 512), F32),
             pltpu.VMEM((4, 4, 4, 2, TOK, 256), F32),
-            pltpu.VMEM((4, 4, INROWS, 512), F32),
+            pltpu.VMEM((4, 4, INROWS, 128), F32),
             pltpu.VMEM((512, 8192), BF16),
-            pltpu.VMEM((4, 2, 2, 32, 192), F32),
-            pltpu.VMEM((3, 2, 2, 32, 192), F32),
-            pltpu.VMEM((3, 32, 192), F32),
+            pltpu.VMEM((4, 2, 32, 384), F32),
+            pltpu.VMEM((3, 2, 32, 384), F32),
+            pltpu.VMEM((3, 32, 256), F32),
             dma((6,)),
             dma((160,)), dma((160,)),
             dma((2, 7)), dma((2, 7)),

time: 110 us -> 103 us (0.936); the launches traced: 109 us -> 101 us
  Pallas kernels: 108 us -> 99.6 us
    pallas_call x1, Pallas kernels: 108 us -> 99.6 us  [body(): pl.pallas_call(kernel, out_shape=jax.ShapeDtypeStruct((64, 192), F32), in...]
where the time goes in v3:
time: 103 us; the launch traced here: 101 us
  Pallas kernels  99.6 us (97%)
  local copies, waits for them, and re-layouts  1.47 us (1%)
    pallas_call x1, Pallas kernels, body(): pl.pallas_call(kernel, out_shape=jax.ShapeDtypeStruct((64, 192), F32), in...  99.6 us

profile of v3, /device:TPU:27, one launch (start us, length us, event | category | flops | bytes accessed | tf_op | source)
XLA Modules:
  0.0 101.1 jit_solution(4866009345892715168)
XLA Ops:
  0.0 99.6 %shard_map.82 = f32[64,192]{1,0:T(8,128)} custom-call(bf16[512,1024]{1,0:T(8,128)(2,1)} %li_hbm.1, bf16[512,1024]{1,0:T(8,128)(2,1)} %og_hbm.1, bf16[1024,256]{1,0:T(8,128)(2,1)} %pi_hbm.1, bf16[1024,256]{1,0:T(8,128)(2,1)} %po_hbm.1, f32[1,8192]{1,0:T(1,128)} %bitcast.1, f32[192,8192]{1,0:T(8,128)} %st_hbm.1, s32[1,16]{1,0:T(1,128)} %len_ref.1, s32[1,16]{1,0:T(1,128)} %ord_ref.1), custom_call_target="tpu_custom_call" | custom-call | tf_op jit(solution)/shard_map/pallas_call | solution.py:463
  99.6 1.5 %copy.10 = f32[64,192]{1,0:T(8,128)} copy(f32[64,192]{1,0:T(8,128)} %shard_map.82) | data formatting | bytes 98304

commit v4 on v3

--- a/solution.py
+++ b/solution.py
@@ -71,9 +71,9 @@
         for sign in (1, -1):
             zlo, zhi = zz(z - sign * (k - 1))
             cols = slice(None) if k < 4 else pl.ds(0 if sign > 0 else 128, 128)
-            deps = ["g"] if k == 1 else [ring(k - 1, sign, "Cz")]
+            deps = ["gc"] if k == 1 else [ring(k - 1, sign, "Cz")]
             add(ring(k, sign, "Cz"), deps, kc if k < 4 else kc / 2, "z", sign, grads.at[y, zlo, x, zhi, crows, cols])
-    call = ["g"] + around("Cz")
+    call = ["gc"] + around("Cz")
     for hop in (1, -1, 2):
         add(f"Ax{hop}", ["g"], ka, "x", hop, grads.at[y, lo, x, hi, A0:B0, :])
     aall = ["g"] + [f"Ax{h}" for h in (1, -1, 2)]
@@ -81,11 +81,15 @@
         add(f"By{hop}", ["g"], kb, "y", hop, gb(z, y, x))
     for hop in (1, -1, 2):
         add(f"Ay{hop}", aall, 4 * ka, "y", hop, ga(z, y))
-    for sign in (1, -1):
-        add(f"Cx{sign}", call, 8 * kc, "x", sign, gz(x, y, crows))
+    crossed = {s: [f"Cx{s},{d}" for d in (0, -1, 1, -2, 2, -3, 3, 4)] for s in (1, -1)}
+    for d in (0, -1, 1, -2, 2, -3, 3, 4):
+        deps = ["gc"] if d == 0 else (["Cz4", "Cz-4"] if d == 4 else [f"Cz{-d}"])
+        zlo, zhi = zz(z + d)
+        for sign in (1, -1):
+            add(f"Cx{sign},{d}", deps, kc, "x", sign, grads.at[y, zlo, x, zhi, crows, :])
     for sign in (1, -1):
         half = first if sign > 0 else second
-        add(f"Cx{2 * sign}", [f"Cx{sign}"], 4 * kc, "x", sign, gz(x - sign, y, crows, half))
+        add(f"Cx{2 * sign}", crossed[sign], 4 * kc, "x", sign, gz(x - sign, y, crows, half))
     for k in (1, 2, 3):
         add(f"Iz{k}", ["i", "Cz3", "Cz-3"], 68, "i", k, ins.at[y, lo])
     iall = ["i"] + [f"Iz{k}" for k in (1, 2, 3)]
@@ -94,7 +98,7 @@
     for r in (*NEAR, FAR):
         tag = f"B{r}z"
         here = ["g"] if r == 0 else [f"By{from_y[r]}"]
-        held = ["A0z1", "A0z-1"] if r == FAR else []
+        held = ["B0z3", "B0z-3"] if r == FAR else []
         for k in (1, 2, 3, 4):
             for sign in (1, -1):
                 deps = here + held if k == 1 else [ring(k - 1, sign, tag)]
@@ -122,7 +126,7 @@
             brought += came[sign] + [f"B{r}x{2 * sign}"]
         tag = f"A{r}z"
         here = aall if r == 0 else [f"Ay{from_y[r]}"]
-        held = ["A1z3", "A-1z3"] if r == FAR else ["B1z3", "B1z-3"]
+        held = ["A0z3", "A0z-3"] if r == FAR else ["B1z3", "B1z-3"]
         for k in (1, 2, 3, 4):
             for sign in (1, -1):
                 deps = here + held if k == 1 else [ring(k - 1, sign, tag)]
@@ -131,14 +135,14 @@
                 add(ring(k, sign, tag), deps, 4 * ka if k < 4 else 2 * ka, "z", sign, ref)
         needs[r] = ball + brought + here + around(tag)
         if r == 0:
-            needs[r] += call + ["Cx1", "Cx-1", "Cx2", "Cx-2"] + iall
+            needs[r] += call + crossed[1] + crossed[-1] + ["Cx2", "Cx-2"] + iall
             for d in (0, -1, 1, -2, 2, -3, 3, 4):
-                deps = ["g"] if d == 0 else (["Cz4", "Cz-4"] if d == 4 else [f"Cz{-d}"])
+                deps = ["gc"] if d == 0 else (["Cz4", "Cz-4"] if d == 4 else [f"Cz{-d}"])
                 zlo, zhi = zz(z + d)
                 for sign in (1, -1):
                     add(f"C0y{sign},{d}", deps, kc, "y", sign, grads.at[y, zlo, x, zhi, crows, :])
             for d in (-1, 1, 2):
-                deps = ["Cx2", "Cx-2"] if d == 2 else [f"Cx{-d}"]
+                deps = ["Cx2", "Cx-2"] if d == 2 else crossed[-d]
                 for sign in (1, -1):
                     add(f"C{d}y{sign}", deps, 8 * kc, "y", sign, gz(x + d, y, crows))
             for sign in (1, -1):
@@ -151,7 +155,11 @@
                 half = first if sign > 0 else second
                 add(f"Iy{2 * sign}", [f"Iy{sign}", f"C2y{sign}"], 136, "y", sign, ins.at[(y - sign) % NY, half])
                 needs[r] += [f"Iy{2 * sign}"]
-            for d in (0, -1, 1, 2):
+            for sign in (1, -1):
+                half = first if sign > 0 else second
+                add(f"C2x{sign}", [f"C{-sign}y{2 * sign}"], 4 * kc, "x", sign, gz(x - sign, y + FAR, crows, half))
+                needs[r] += [f"C2x{sign}"]
+            for d in (-1, 1, 0):
                 for sign in (1, -1):
                     half = first if sign > 0 else second
                     deps = (across[sign] if d == 0 else [f"C{d}y{sign}"]) + [f"C1y{sign}"]
@@ -171,10 +179,10 @@
     return device(x, y, (z // 4) * 4 + (z % 4 + m.hop) % 4, c)
 
 
-def order_of(plan, tasks, rate=38.0, latency=2.0, late=4.0):
-    free, got, sent, events, steps = {}, set(), set(), [(0.0, 0, "g"), (late, 1, "i")], []
+def order_of(plan, tasks, rate=38.0, latency=2.0, late=5.0):
+    free, got, sent, events, steps = {}, set(), set(), [(0.0, 0, "gc"), (1.2, 1, "g"), (late, 2, "i")], []
     heapq.heapify(events)
-    count, now, todo, idle = 2, 0.0, list(tasks), 0.0
+    count, now, todo = 3, 0.0, list(tasks)
     while events or todo:
         ready = next((t for t in todo if all(d in got for d in t[1])), None)
         if ready and not (events and events[0][0] <= now):
@@ -220,9 +228,6 @@
     )
 
 
-RS = ("R1", "L1", "R1b", "L1b", "R2", "L2", "Z")
-
-
 def kernel(
     li_hbm, og_hbm, pi_hbm, po_hbm, inv_hbm, st_hbm, len_ref, ord_ref, out_ref,
     li, og, pi, po, inv, raw, st_hi, st_lo, pg, pin, rg, rin, grads, ins, q, sc, rsc, fin,
@@ -265,10 +270,17 @@
             "R1": one(0, buf.at[xo, 0], right), "L1": one(1, buf.at[xo, 1], left),
             "R1b": one(2, buf.at[xr, 1], right), "L1b": one(3, buf.at[xl, 0], left),
             "R2": one(4, buf.at[xr, 0], right), "L2": one(5, buf.at[xl, 1], left),
-            "Z": one(6, buf.at[x, 1 - zhi], device(x, y, z + 4, c)),
         }
 
+    def over(n, k, buf, got, rows):
+        src, dst = buf.at[x, 1 - zhi, rows], got.at[6, rows]
+        return remote(src, dst, rsend.at[n, k], rrecv.at[n, k], device(x, y, z + 4, c))
+
     first, second = reduce_plan(0, pg, rg), reduce_plan(1, pin, rin)
+    early, later = slice(C0, TOK), slice(0, C0)
+    first["Zc"] = over(0, 6, pg, rg, early)
+    first["Z"] = over(0, 7, pg, rg, later)
+    second["Z"] = over(1, 6, pin, rin, slice(0, 32))
 
     loads[0].wait()
     loads[1].wait()
@@ -281,10 +293,6 @@
     pin[...] = lax.dot_general(
         pi[...], li[...], (((0,), (1,)), ((), ())), preferred_element_type=F32
     ).reshape(pin.shape)
-    for k in ("R1", "L1", "R1b", "L1b"):
-        second[k].start()
-    loads[5].start()
-    swap.start()
 
     position = lax.broadcasted_iota(jnp.int32, (8, 128), 0) * 128 + lax.broadcasted_iota(jnp.int32, (8, 128), 1)
     slots, begin = jnp.zeros((8, 128), F32), jnp.int32(0)
@@ -306,13 +314,20 @@
     def reduced(cps, buf, got):
         for k in ("R1b", "L1b", "R2", "L2"):
             cps[k].wait_recv()
-        buf[x, 0] = buf[x, 0] + (got[3] + got[4])
-        buf[x, 1] = buf[x, 1] + (got[2] + got[5])
-        cps["Z"].start()
+        for half in (1 - zhi, zhi):
+            buf[x, half] = buf[x, half] + (got[3 - half] + got[4 + half])
+            if half is not zhi:
+                for k in ("Zc", "Z"):
+                    if k in cps:
+                        cps[k].start()
 
     halfway(first, pg, rg)
+    for k in ("R1", "L1", "R1b", "L1b"):
+        second[k].start()
+    loads[5].start()
+    swap.start()
+    reduced(first, pg, rg)
     halfway(second, pin, rin)
-    reduced(first, pg, rg)
     reduced(second, pin, rin)
 
     plan, needs = gather_plan(me, grads, ins)
@@ -410,9 +425,12 @@
         run[f"outer{FAR},{n}"] = (outer, (FAR, n))
 
     for verb, name in order_of(plan, tasks)[0]:
-        if name == "g":
+        if name == "gc":
+            first["Zc"].wait_recv()
+            grads[y, zlo, x, zhi, early] = pg[x, zhi, early] + rg[6, early]
+        elif name == "g":
             first["Z"].wait_recv()
-            grads[y, zlo, x, zhi] = pg[x, zhi] + rg[6]
+            grads[y, zlo, x, zhi, later] = pg[x, zhi, later] + rg[6, later]
         elif name == "i":
             second["Z"].wait_recv()
             whole = pin[x, zhi] + rin[6]
@@ -427,6 +445,8 @@
             work(*given)
     far_scores()
     pass_on(FAR)
+    for copy in (*first.values(), *second.values(), *copies.values()):
+        copy.wait_send()
 
     sends = [
         remote(sc.at[x], rsc.at[n], ssend.at[n], srecv.at[n], right) for n in range(3)
@@ -453,7 +473,7 @@
         out_ref[pl.ds(pl.multiple_of(half * 32 + c * QB, QB), QB), :] = mine[part]
         out_ref[pl.ds(pl.multiple_of(half * 32 + (1 - c) * QB, QB), QB), :] = theirs[part]
 
-    for copy in (*first.values(), *second.values(), *copies.values(), *sends, *ends):
+    for copy in (*sends, *ends):
         copy.wait_send()
 
 
@@ -485,8 +505,8 @@
             pltpu.VMEM((3, 2, 32, 384), F32),
             pltpu.VMEM((3, 32, 256), F32),
             dma((6,)),
-            dma((160,)), dma((160,)),
-            dma((2, 7)), dma((2, 7)),
+            dma((176,)), dma((176,)),
+            dma((2, 8)), dma((2, 8)),
             dma((3,)), dma((3,)),
             dma((4,)), dma((4,)),
         ],

time: 103 us -> 100 us (0.971); the launches traced: 101 us -> 99.9 us
  Pallas kernels: 99.6 us -> 98.4 us
    pallas_call x1, Pallas kernels: 99.6 us -> 98.4 us  [body(): pl.pallas_call(kernel, out_shape=jax.ShapeDtypeStruct((64, 192), F32), in...]
where the time goes in v4:
time: 100 us; the launch traced here: 99.9 us
  Pallas kernels  98.4 us (98%)
  local copies, waits for them, and re-layouts  1.47 us (1%)
    pallas_call x1, Pallas kernels, body(): pl.pallas_call(kernel, out_shape=jax.ShapeDtypeStruct((64, 192), F32), in...  98.4 us

profile of v4, /device:TPU:27, one launch (start us, length us, event | category | flops | bytes accessed | tf_op | source)
XLA Modules:
  0.0 99.9 jit_solution(14651966340708300875)
XLA Ops:
  0.0 98.4 %shard_map.82 = f32[64,192]{1,0:T(8,128)} custom-call(bf16[512,1024]{1,0:T(8,128)(2,1)} %li_hbm.1, bf16[512,1024]{1,0:T(8,128)(2,1)} %og_hbm.1, bf16[1024,256]{1,0:T(8,128)(2,1)} %pi_hbm.1, bf16[1024,256]{1,0:T(8,128)(2,1)} %po_hbm.1, f32[1,8192]{1,0:T(1,128)} %bitcast.1, f32[192,8192]{1,0:T(8,128)} %st_hbm.1, s32[1,16]{1,0:T(1,128)} %len_ref.1, s32[1,16]{1,0:T(1,128)} %ord_ref.1), custom_call_target="tpu_custom_call" | custom-call | tf_op jit(solution)/shard_map/pallas_call | solution.py:483
  98.4 1.5 %copy.10 = f32[64,192]{1,0:T(8,128)} copy(f32[64,192]{1,0:T(8,128)} %shard_map.82) | data formatting | bytes 98304

commit v5 on v4

--- a/solution.py
+++ b/solution.py
@@ -179,7 +179,7 @@
     return device(x, y, (z // 4) * 4 + (z % 4 + m.hop) % 4, c)
 
 
-def order_of(plan, tasks, rate=38.0, latency=2.0, late=5.0):
+def order_of(plan, tasks, rate=32.0, latency=2.0, late=5.0):
     free, got, sent, events, steps = {}, set(), set(), [(0.0, 0, "gc"), (1.2, 1, "g"), (late, 2, "i")], []
     heapq.heapify(events)
     count, now, todo = 3, 0.0, list(tasks)
@@ -418,7 +418,7 @@
         run[f"near{n}"] = (near_scores, (n,))
         done.append(f"near{n}")
     for r in NEAR:
-        tasks.append((f"pass{r}", tuple(done), 0.1))
+        tasks.append((f"pass{r}", tuple(done) + tuple(needs[FAR]), 0.1))
         run[f"pass{r}"] = (pass_on, (r,))
     for n in range(2):
         tasks.append((f"outer{FAR},{n}", tuple(done) + tuple(needs[FAR]), 1.3))

time: 100 us -> 99.5 us (level); the launches traced: 99.9 us -> 97.8 us
  Pallas kernels: 98.4 us -> 96.3 us
    pallas_call x1, Pallas kernels: 98.4 us -> 96.3 us  [body(): pl.pallas_call(kernel, out_shape=jax.ShapeDtypeStruct((64, 192), F32), in...]
where the time goes in v5:
time: 99.5 us; the launch traced here: 97.8 us
  Pallas kernels  96.3 us (97%)
  local copies, waits for them, and re-layouts  1.47 us (1%)
    pallas_call x1, Pallas kernels, body(): pl.pallas_call(kernel, out_shape=jax.ShapeDtypeStruct((64, 192), F32), in...  96.3 us

profile of v5, /device:TPU:27, one launch (start us, length us, event | category | flops | bytes accessed | tf_op | source)
XLA Modules:
  0.0 97.8 jit_solution(417309466828520285)
XLA Ops:
  0.0 96.3 %shard_map.82 = f32[64,192]{1,0:T(8,128)} custom-call(bf16[512,1024]{1,0:T(8,128)(2,1)} %li_hbm.1, bf16[512,1024]{1,0:T(8,128)(2,1)} %og_hbm.1, bf16[1024,256]{1,0:T(8,128)(2,1)} %pi_hbm.1, bf16[1024,256]{1,0:T(8,128)(2,1)} %po_hbm.1, f32[1,8192]{1,0:T(1,128)} %bitcast.1, f32[192,8192]{1,0:T(8,128)} %st_hbm.1, s32[1,16]{1,0:T(1,128)} %len_ref.1, s32[1,16]{1,0:T(1,128)} %ord_ref.1), custom_call_target="tpu_custom_call" | custom-call | tf_op jit(solution)/shard_map/pallas_call | solution.py:483
  96.4 1.5 %copy.10 = f32[64,192]{1,0:T(8,128)} copy(f32[64,192]{1,0:T(8,128)} %shard_map.82) | data formatting | bytes 98304

commit v6 on v5

--- a/solution.py
+++ b/solution.py
@@ -405,7 +405,7 @@
         def _():
             remote(sc.at[to], rsc.at[slot], ssend.at[slot], srecv.at[slot], device(to, y, z, c)).start()
 
-    tasks = [(f"prepare{n}", (), 0.6) for n in range(4)]
+    tasks = [(f"prepare{n}", ("A0z1",), 0.6) for n in range(4)]
     run = {f"prepare{n}": (prepare, (n,)) for n in range(4)}
     done = [f"prepare{n}" for n in range(4)]
     for r in NEAR:

time: 99.5 us -> 99.2 us (level)
  no operation moved by 1% of the time
where the time goes in v6:
time: 99.2 us; the launch traced here: 98.3 us
  Pallas kernels  96.9 us (98%)
  local copies, waits for them, and re-layouts  1.47 us (1%)
    pallas_call x1, Pallas kernels, body(): pl.pallas_call(kernel, out_shape=jax.ShapeDtypeStruct((64, 192), F32), in...  96.9 us

profile of v6, /device:TPU:27, one launch (start us, length us, event | category | flops | bytes accessed | tf_op | source)
XLA Modules:
  0.0 98.3 jit_solution(2106643151383948071)
XLA Ops:
  0.0 96.9 %shard_map.82 = f32[64,192]{1,0:T(8,128)} custom-call(bf16[512,1024]{1,0:T(8,128)(2,1)} %li_hbm.1, bf16[512,1024]{1,0:T(8,128)(2,1)} %og_hbm.1, bf16[1024,256]{1,0:T(8,128)(2,1)} %pi_hbm.1, bf16[1024,256]{1,0:T(8,128)(2,1)} %po_hbm.1, f32[1,8192]{1,0:T(1,128)} %bitcast.1, f32[192,8192]{1,0:T(8,128)} %st_hbm.1, s32[1,16]{1,0:T(1,128)} %len_ref.1, s32[1,16]{1,0:T(1,128)} %ord_ref.1), custom_call_target="tpu_custom_call" | custom-call | tf_op jit(solution)/shard_map/pallas_call | solution.py:483
  96.9 1.5 %copy.10 = f32[64,192]{1,0:T(8,128)} copy(f32[64,192]{1,0:T(8,128)} %shard_map.82) | data formatting | bytes 98304
